TPU v7x, 32 devices: a whole 2x2x4 slice. The times are simulated.
32 devices in a mesh: seq: 4 (over x, core), nbr: 8 (over z, y).
Axes of the slice: x: 2, y: 2, z: 4, core: 2. Of those that a mesh axis runs over, the one named last changes fastest.
Arguments:
- tokens: bfloat16 [32, 256, 768], P(('seq', 'nbr')), may hold values from -6 to 6
- neighbours: bfloat16 [256, 128, 768], P(('seq', 'nbr')), may hold values from -6 to 6
- out_grad: bfloat16 [32, 256, 768], P(('seq', 'nbr')), may hold values from -6 to 6
- lengths: int32 [32], P(('seq', 'nbr')), may hold values from 64 to 256, as said below
- slot_order: int32 [32, 8], P(('seq', 'nbr')), may hold values from 0 to 7, each once within a row
- selfgain: float32 [768], replicated, may hold values from 0.1 to 1.9
- selfjoint: bfloat16 [768, 2304], replicated, may hold values from -0.21875 to 0.21875
- selfmerge: bfloat16 [768, 768], replicated, may hold values from -0.875 to 0.875
- crossgain: float32 [768], replicated, may hold values from 0.1 to 1.9
- crossquery: bfloat16 [768, 768], replicated, may hold values from -0.21875 to 0.21875
- crossmerge: bfloat16 [768, 768], replicated, may hold values from -0.875 to 0.875
- feedgain: float32 [768], replicated, may hold values from 0.1 to 1.9
- feedup: bfloat16 [768, 3072], replicated, may hold values from -0.21875 to 0.21875
- feeddown: bfloat16 [3072, 768], replicated, may hold values from -0.109375 to 0.109375
- codergain: float32 [768], replicated, may hold values from 0.1 to 1.9
- coderjoint: bfloat16 [768, 2304], replicated, may hold values from -0.21875 to 0.21875
- codermerge: bfloat16 [768, 768], replicated, may hold values from -0.875 to 0.875
- codermid: float32 [768], replicated, may hold values from 0.1 to 1.9
- coderup: bfloat16 [768, 3072], replicated, may hold values from -0.21875 to 0.21875
- coderdown: bfloat16 [3072, 768], replicated, may hold values from -0.109375 to 0.109375
- codertop: float32 [768], replicated, may hold values from 0.1 to 1.9
- memorymap: bfloat16 [768, 1536], replicated, may hold values from -0.21875 to 0.21875
Outputs:
- output: bfloat16 [32, 256, 768], P(('seq', 'nbr'))
- input_grad: float32 [32, 256, 768], P(('seq', 'nbr'))
- grad_selfgain: float32 [768], P('nbr')
- grad_selfjoint: float32 [768, 2304], P('nbr')
- grad_selfmerge: float32 [768, 768], P('nbr')
- grad_crossgain: float32 [768], P('nbr')
- grad_crossquery: float32 [768, 768], P('nbr')
- grad_crossmerge: float32 [768, 768], P('nbr')
- grad_feedgain: float32 [768], P('nbr')
- grad_feedup: float32 [768, 3072], P('nbr')
- grad_feeddown: float32 [3072, 768], P('nbr')
- grad_codergain: float32 [768], P('nbr')
- grad_coderjoint: float32 [768, 2304], P('nbr')
- grad_codermerge: float32 [768, 768], P('nbr')
- grad_codermid: float32 [768], P('nbr')
- grad_coderup: float32 [768, 3072], P('nbr')
- grad_coderdown: float32 [3072, 768], P('nbr')
- grad_codertop: float32 [768], P('nbr')
- grad_memorymap: float32 [768, 1536], P('nbr')
Inputs may be any that keep to these rules, and one draw needn't show every extreme that they name: `lengths`: some sequence has exactly 256 tokens in every draw. `slot_order`: each row is a permutation of its 8 places.
All inputs are finite; a program needn't handle non-finite values.
Results may differ from a plain program's by a relative error of at most 0.025.
Values may be sent and summed in bfloat16 or wider, within the bound.
A program may use at most 256 MiB of HBM per device.

v0:
```python
from functools import partial

import jax
import jax.numpy as jnp
from jax import lax
from jax.sharding import PartitionSpec as P

D = 768
HEADS = 12
HD = 64
CH = 64


def norm_forward(values, gain):
    centred = values - jnp.mean(values, axis=-1, keepdims=True)
    inverse = lax.rsqrt(jnp.mean(centred * centred, axis=-1, keepdims=True) + 1e-05)
    normed = centred * inverse
    return ((normed * gain).astype(jnp.bfloat16), normed, inverse)


def norm_backward(grad, normed, inverse, gain):
    gain_grad = jnp.sum((grad * normed).reshape(-1, normed.shape[-1]), axis=0)
    scaled = grad * gain
    inner = jnp.mean(scaled * normed, axis=-1, keepdims=True)
    result = inverse * (scaled - jnp.mean(scaled, axis=-1, keepdims=True) - normed * inner)
    return (result, gain_grad)


def times(values, weight):
    return jnp.einsum("...k,kn->...n", values, weight, preferred_element_type=jnp.float32)


def times_back(grad, weight):
    return jnp.einsum("...n,kn->...k", grad, weight, preferred_element_type=jnp.float32)


def weight_grad(values, grad):
    flat_values = values.reshape(-1, values.shape[-1])
    flat_grad = grad.reshape(-1, grad.shape[-1])
    return lax.dot_general(
        flat_values, flat_grad, (((0,), (0,)), ((), ())), preferred_element_type=jnp.float32
    )


def curve_grad(rising, upstream):
    return jax.vjp(partial(jax.nn.gelu, approximate=True), rising)[1](upstream)[0]


def heads(joint, index):
    piece = joint[..., index * D : (index + 1) * D]
    return piece.reshape(piece.shape[:-1] + (HEADS, HD))


def flatten(values):
    return values.reshape(values.shape[:-2] + (D,))


def attend_forward(queries, keys, values, allowed):
    products = jnp.einsum("brhd,bshd->bhrs", queries, keys, preferred_element_type=jnp.float32)
    scores = jnp.where(allowed, products * HD ** (-0.5), -1000000000.0)
    highest = jnp.max(scores, axis=-1, keepdims=True)
    exponent = jnp.exp(scores - highest)
    totals = jnp.sum(exponent, axis=-1, keepdims=True)
    probs = (exponent / totals).astype(jnp.bfloat16)
    mixed = jnp.einsum("bhrs,bshd->brhd", probs, values, preferred_element_type=jnp.float32)
    return (flatten(mixed).astype(jnp.bfloat16), highest + jnp.log(totals))


def attend_backward(queries, keys, values, allowed, logsum, grad_mixed):
    outgoing = grad_mixed.reshape(queries.shape)
    products = jnp.einsum("brhd,bshd->bhrs", queries, keys, preferred_element_type=jnp.float32)
    scores = jnp.where(allowed, products * HD ** (-0.5), -1000000000.0)
    probs = jnp.exp(scores - logsum)
    value_grad = jnp.einsum(
        "bhrs,brhd->bshd", probs.astype(jnp.bfloat16), outgoing, preferred_element_type=jnp.float32
    )
    prob_grad = jnp.einsum("brhd,bshd->bhrs", outgoing, values, preferred_element_type=jnp.float32)
    score_grad = probs * (prob_grad - jnp.sum(probs * prob_grad, axis=-1, keepdims=True))
    rounded = (score_grad * HD ** (-0.5)).astype(jnp.bfloat16)
    query_grad = jnp.einsum("bhrs,bshd->brhd", rounded, keys, preferred_element_type=jnp.float32)
    key_grad = jnp.einsum("bhrs,brhd->bshd", rounded, queries, preferred_element_type=jnp.float32)
    return (flatten(query_grad), flatten(key_grad), flatten(value_grad))


def encode_forward(block, params):
    (
        bottom_gain,
        joint_weight,
        merge_weight,
        middle_gain,
        up_weight,
        down_weight,
        top_gain,
        memory_weight,
    ) = params
    embedded = block.astype(jnp.float32)
    normed_a, plain_a, inverse_a = norm_forward(embedded, bottom_gain)
    joint = times(normed_a, joint_weight).astype(jnp.bfloat16)
    queries, keys, values = (heads(joint, 0), heads(joint, 1), heads(joint, 2))
    everywhere = jnp.ones((1, 1, 1, 1), jnp.bool_)
    mixed, logsum = attend_forward(queries, keys, values, everywhere)
    middle = embedded + times(mixed, merge_weight)
    normed_b, plain_b, inverse_b = norm_forward(middle, middle_gain)
    rising = times(normed_b, up_weight)
    hidden = jax.nn.gelu(rising, approximate=True).astype(jnp.bfloat16)
    upper = middle + times(hidden, down_weight)
    normed_c, plain_c, inverse_c = norm_forward(upper, top_gain)
    memory = times(normed_c, memory_weight).astype(jnp.bfloat16)
    kept = (
        normed_a,
        plain_a,
        queries,
        keys,
        values,
        logsum,
        mixed,
        normed_b,
        plain_b,
        inverse_b,
        rising,
        hidden,
        normed_c,
        plain_c,
        inverse_c,
    )
    return (memory, kept)


def encode_backward(memory_grad, kept, params):
    (
        bottom_gain,
        joint_weight,
        merge_weight,
        middle_gain,
        up_weight,
        down_weight,
        top_gain,
        memory_weight,
    ) = params
    (
        normed_a,
        plain_a,
        queries,
        keys,
        values,
        logsum,
        mixed,
        normed_b,
        plain_b,
        inverse_b,
        rising,
        hidden,
        normed_c,
        plain_c,
        inverse_c,
    ) = kept
    memory_weight_grad = weight_grad(normed_c, memory_grad)
    upper_total, top_gain_grad = norm_backward(
        times_back(memory_grad, memory_weight), plain_c, inverse_c, top_gain
    )
    down_input = upper_total.astype(jnp.bfloat16)
    down_weight_grad = weight_grad(hidden, down_input)
    rising_grad = curve_grad(rising, times_back(down_input, down_weight)).astype(jnp.bfloat16)
    up_weight_grad = weight_grad(normed_b, rising_grad)
    middle_part, middle_gain_grad = norm_backward(
        times_back(rising_grad, up_weight), plain_b, inverse_b, middle_gain
    )
    merge_input = (upper_total + middle_part).astype(jnp.bfloat16)
    merge_weight_grad = weight_grad(mixed, merge_input)
    mixed_grad = times_back(merge_input, merge_weight).astype(jnp.bfloat16)
    everywhere = jnp.ones((1, 1, 1, 1), jnp.bool_)
    query_grad, key_grad, value_grad = attend_backward(
        queries, keys, values, everywhere, logsum, mixed_grad
    )
    joint_grad = jnp.concatenate([query_grad, key_grad, value_grad], axis=-1).astype(jnp.bfloat16)
    joint_weight_grad = weight_grad(normed_a, joint_grad)
    bottom_gain_grad = jnp.sum(
        (times_back(joint_grad, joint_weight) * plain_a).reshape(-1, D), axis=0
    )
    return (
        bottom_gain_grad,
        joint_weight_grad,
        merge_weight_grad,
        middle_gain_grad,
        up_weight_grad,
        down_weight_grad,
        top_gain_grad,
        memory_weight_grad,
    )


def decode_both(tokens, out_grad, length, order, memory, params):
    (
        self_gain,
        self_joint,
        self_merge,
        cross_gain,
        cross_query,
        cross_merge,
        feed_gain,
        feed_up,
        feed_down,
    ) = params
    sequence = tokens[0].astype(jnp.float32)
    rows = sequence.shape[0]
    places = jnp.arange(rows, dtype=jnp.int32)
    normed_a, plain_a, inverse_a = norm_forward(sequence, self_gain)
    joint = times(normed_a, self_joint).astype(jnp.bfloat16)[None]
    queries, keys, values = (heads(joint, 0), heads(joint, 1), heads(joint, 2))
    causal = ((places[None, :] <= places[:, None]) & (places[None, :] < length))[None, None]
    mixed, logsum = attend_forward(queries, keys, values, causal)
    after_self = sequence + times(mixed[0], self_merge)
    normed_b, plain_b, inverse_b = norm_forward(after_self, cross_gain)
    span_count = order.shape[0] // 2
    asked = times(normed_b, cross_query).astype(jnp.bfloat16).reshape(span_count, -1, HEADS, HD)
    chosen = memory[order].reshape(span_count, -1, 2 * D)
    memory_keys = chosen[..., :D].reshape(span_count, -1, HEADS, HD)
    memory_values = chosen[..., D:].reshape(span_count, -1, HEADS, HD)
    everywhere = jnp.ones((1, 1, 1, 1), jnp.bool_)
    crossed, cross_logsum = attend_forward(asked, memory_keys, memory_values, everywhere)
    crossed = crossed.reshape(rows, D)
    live = (places // CH * CH < length).astype(jnp.float32)[:, None]
    after_cross = after_self + times(crossed, cross_merge) * live
    normed_c, plain_c, inverse_c = norm_forward(after_cross, feed_gain)
    rising = times(normed_c, feed_up)
    hidden = jax.nn.gelu(rising, approximate=True).astype(jnp.bfloat16)
    output = (after_cross + times(hidden, feed_down)).astype(jnp.bfloat16)[None]
    upstream = out_grad[0].astype(jnp.float32)
    down_input = out_grad[0]
    feed_down_grad = weight_grad(hidden, down_input)
    rising_grad = curve_grad(rising, times_back(down_input, feed_down)).astype(jnp.bfloat16)
    feed_up_grad = weight_grad(normed_c, rising_grad)
    part_c, feed_gain_grad = norm_backward(
        times_back(rising_grad, feed_up), plain_c, inverse_c, feed_gain
    )
    cross_total = upstream + part_c
    cross_input = (cross_total * live).astype(jnp.bfloat16)
    cross_merge_grad = weight_grad(crossed, cross_input)
    crossed_grad = times_back(cross_input, cross_merge).astype(jnp.bfloat16)
    asked_grad, key_grad, value_grad = attend_backward(
        asked, memory_keys, memory_values, everywhere, cross_logsum, crossed_grad
    )
    asked_grad = asked_grad.reshape(rows, D).astype(jnp.bfloat16)
    chosen_grad = jnp.concatenate([key_grad, value_grad], axis=-1).reshape(memory.shape)
    memory_grad = (
        jnp.zeros(memory.shape, jnp.float32).at[order].set(chosen_grad).astype(jnp.bfloat16)
    )
    cross_query_grad = weight_grad(normed_b, asked_grad)
    part_b, cross_gain_grad = norm_backward(
        times_back(asked_grad, cross_query), plain_b, inverse_b, cross_gain
    )
    self_total = cross_total + part_b
    self_input = self_total.astype(jnp.bfloat16)
    self_merge_grad = weight_grad(mixed[0], self_input)
    mixed_grad = times_back(self_input, self_merge).astype(jnp.bfloat16)[None]
    query_grad, key_grad_s, value_grad_s = attend_backward(
        queries, keys, values, causal, logsum, mixed_grad
    )
    joint_grad = jnp.concatenate([query_grad, key_grad_s, value_grad_s], axis=-1)[0].astype(
        jnp.bfloat16
    )
    self_joint_grad = weight_grad(normed_a, joint_grad)
    part_a, self_gain_grad = norm_backward(
        times_back(joint_grad, self_joint), plain_a, inverse_a, self_gain
    )
    input_grad = (self_total + part_a)[None]
    decoder_grads = (
        self_gain_grad,
        self_joint_grad,
        self_merge_grad,
        cross_gain_grad,
        cross_query_grad,
        cross_merge_grad,
        feed_gain_grad,
        feed_up_grad,
        feed_down_grad,
    )
    return (output, input_grad, decoder_grads, memory_grad)


def body(
    tokens,
    neighbours,
    out_grad,
    lengths,
    slot_order,
    selfgain,
    selfjoint,
    selfmerge,
    crossgain,
    crossquery,
    crossmerge,
    feedgain,
    feedup,
    feeddown,
    codergain,
    coderjoint,
    codermerge,
    codermid,
    coderup,
    coderdown,
    codertop,
    memorymap,
):
    decoder_params = (
        selfgain,
        selfjoint,
        selfmerge,
        crossgain,
        crossquery,
        crossmerge,
        feedgain,
        feedup,
        feeddown,
    )
    encoder_params = (
        codergain,
        coderjoint,
        codermerge,
        codermid,
        coderup,
        coderdown,
        codertop,
        memorymap,
    )
    own_memory, encoder_kept = encode_forward(neighbours, encoder_params)
    memory = lax.all_to_all(own_memory, "seq", split_axis=0, concat_axis=0, tiled=True)
    output, input_grad, decoder_grads, memory_grad = decode_both(
        tokens, out_grad, lengths[0], slot_order[0], memory, decoder_params
    )
    returned = lax.all_to_all(memory_grad, "seq", split_axis=0, concat_axis=0, tiled=True)
    encoder_grads = encode_backward(returned, encoder_kept, encoder_params)
    local = decoder_grads + encoder_grads
    combined = (
        lax.psum_scatter(
            local[0].astype(jnp.bfloat16), "nbr", scatter_dimension=0, tiled=True
        ).astype(jnp.float32),
        lax.psum_scatter(
            local[1].astype(jnp.bfloat16), "nbr", scatter_dimension=0, tiled=True
        ).astype(jnp.float32),
        lax.psum_scatter(
            local[2].astype(jnp.bfloat16), "nbr", scatter_dimension=0, tiled=True
        ).astype(jnp.float32),
        lax.psum_scatter(
            local[3].astype(jnp.bfloat16), "nbr", scatter_dimension=0, tiled=True
        ).astype(jnp.float32),
        lax.psum_scatter(
            local[4].astype(jnp.bfloat16), "nbr", scatter_dimension=0, tiled=True
        ).astype(jnp.float32),
        lax.psum_scatter(
            local[5].astype(jnp.bfloat16), "nbr", scatter_dimension=0, tiled=True
        ).astype(jnp.float32),
        lax.psum_scatter(
            local[6].astype(jnp.bfloat16), "nbr", scatter_dimension=0, tiled=True
        ).astype(jnp.float32),
        lax.psum_scatter(
            local[7].astype(jnp.bfloat16), "nbr", scatter_dimension=0, tiled=True
        ).astype(jnp.float32),
        lax.psum_scatter(
            local[8].astype(jnp.bfloat16), "nbr", scatter_dimension=0, tiled=True
        ).astype(jnp.float32),
        lax.psum_scatter(
            local[9].astype(jnp.bfloat16), "nbr", scatter_dimension=0, tiled=True
        ).astype(jnp.float32),
        lax.psum_scatter(
            local[10].astype(jnp.bfloat16), "nbr", scatter_dimension=0, tiled=True
        ).astype(jnp.float32),
        lax.psum_scatter(
            local[11].astype(jnp.bfloat16), "nbr", scatter_dimension=0, tiled=True
        ).astype(jnp.float32),
        lax.psum_scatter(
            local[12].astype(jnp.bfloat16), "nbr", scatter_dimension=0, tiled=True
        ).astype(jnp.float32),
        lax.psum_scatter(
            local[13].astype(jnp.bfloat16), "nbr", scatter_dimension=0, tiled=True
        ).astype(jnp.float32),
        lax.psum_scatter(
            local[14].astype(jnp.bfloat16), "nbr", scatter_dimension=0, tiled=True
        ).astype(jnp.float32),
        lax.psum_scatter(
            local[15].astype(jnp.bfloat16), "nbr", scatter_dimension=0, tiled=True
        ).astype(jnp.float32),
        lax.psum_scatter(
            local[16].astype(jnp.bfloat16), "nbr", scatter_dimension=0, tiled=True
        ).astype(jnp.float32),
    )
    combined = (
        lax.psum(combined[0].astype(jnp.bfloat16), "seq").astype(jnp.float32),
        lax.psum(combined[1].astype(jnp.bfloat16), "seq").astype(jnp.float32),
        lax.psum(combined[2].astype(jnp.bfloat16), "seq").astype(jnp.float32),
        lax.psum(combined[3].astype(jnp.bfloat16), "seq").astype(jnp.float32),
        lax.psum(combined[4].astype(jnp.bfloat16), "seq").astype(jnp.float32),
        lax.psum(combined[5].astype(jnp.bfloat16), "seq").astype(jnp.float32),
        lax.psum(combined[6].astype(jnp.bfloat16), "seq").astype(jnp.float32),
        lax.psum(combined[7].astype(jnp.bfloat16), "seq").astype(jnp.float32),
        lax.psum(combined[8].astype(jnp.bfloat16), "seq").astype(jnp.float32),
        lax.psum(combined[9].astype(jnp.bfloat16), "seq").astype(jnp.float32),
        lax.psum(combined[10].astype(jnp.bfloat16), "seq").astype(jnp.float32),
        lax.psum(combined[11].astype(jnp.bfloat16), "seq").astype(jnp.float32),
        lax.psum(combined[12].astype(jnp.bfloat16), "seq").astype(jnp.float32),
        lax.psum(combined[13].astype(jnp.bfloat16), "seq").astype(jnp.float32),
        lax.psum(combined[14].astype(jnp.bfloat16), "seq").astype(jnp.float32),
        lax.psum(combined[15].astype(jnp.bfloat16), "seq").astype(jnp.float32),
        lax.psum(combined[16].astype(jnp.bfloat16), "seq").astype(jnp.float32),
    )
    return (output, input_grad) + tuple(combined)


def solution(mesh):
    placed = (
        P(("seq", "nbr"), None, None),
        P(("seq", "nbr"), None, None),
        P(("seq", "nbr"), None, None),
        P(("seq", "nbr")),
        P(("seq", "nbr"), None),
        P(),
        P(),
        P(),
        P(),
        P(),
        P(),
        P(),
        P(),
        P(),
        P(),
        P(),
        P(),
        P(),
        P(),
        P(),
        P(),
        P(),
    )
    return jax.shard_map(
        body,
        mesh=mesh,
        in_specs=placed,
        out_specs=(
            P(("seq", "nbr"), None, None),
            P(("seq", "nbr"), None, None),
            P("nbr"),
            P("nbr", None),
            P("nbr", None),
            P("nbr"),
            P("nbr", None),
            P("nbr", None),
            P("nbr"),
            P("nbr", None),
            P("nbr", None),
            P("nbr"),
            P("nbr", None),
            P("nbr", None),
            P("nbr"),
            P("nbr", None),
            P("nbr", None),
            P("nbr"),
            P("nbr", None),
        ),
        check_vma=False,
    )
```

profile of v0, /device:TPU:0, one launch (start us, length us, event | category | flops | bytes accessed | tf_op | source)
XLA Modules:
  0.0 1204.1 jit_solution(4210692210169763526)
XLA Ops:
  42.3 8.0 fusion.231
  166.1 23.9 %fusion.87 = f32[4,256,12,64]{1,3,2,0:T(8,128)} fusion(bf16[4,64,12,64]{1,3,2,0:T(8,128)(2,1)} %copy.138, f32[4,12,64,256]{3,2,1,0:T(8,128)} %fusion.234, f32[4,12,64,256]{3,2,1,0:T(8,128)} %copy-done.2, f32[4,12,64]{2,1,0:T(8,128)} %copy-done.47), kind=kOutput, calls=%fused_computation.118 | convolution fusion | flops 107744512 | bytes 9842688 | tf_op jit(solution)/shard_map/bhrs,brhd->bshd/dot_general | solution.py:81
  213.8 13.4 %scatter_fusion = f32[8,128,1536]{2,1,0:T(8,128)} fusion(f32[8,128,1536]{2,1,0:T(8,128)} %broadcast_in_dim.53, s32[8]{0:T(128)} %copy-done.95, f32[8,128,1536]{2,1,0:T(8,128)} %pad_maximum_fusion), kind=kCustom, calls=%fused_computation.1 | custom fusion | bytes 18874400 | tf_op jit(solution)/shard_map/scatter | solution.py:246
  232.0 23.2 %fusion.129 = bf16[4,64,12,64]{1,3,2,0:T(8,128)(2,1)} fusion(bf16[4,256,12,64]{1,3,2,0:T(8,128)(2,1)} %bitcast.242, f32[4,12,64,256]{3,2,1,0:T(8,128)} %fusion.234, f32[4,12,64,256]{3,2,1,0:T(8,128)} %copy-done.2, f32[4,12,64]{2,1,0:T(8,128)} %copy-done.47), kind=kOutput, calls=%fused_computation.145 | convolution fusion | flops 107941120 | bytes 8269824 | tf_op jit(solution)/shard_map/bhrs,bshd->brhd/dot_general | solution.py:80
  273.9 31.0 %all-to-all-done.1 = bf16[8,128,1536]{2,1,0:T(8,128)(2,1)} async-done(((bf16[8,128,1536]{2,1,0:T(8,128)(2,1)}), bf16[8,128,1536]{2,1,0:T(8,128)(2,1)}, u32[]{:S(2)}, u32[]{:S(2)}) %all-to-all-start.1) | async-done | bytes 3145760 | tf_op jit(solution)/shard_map/all_to_all | solution.py:331
  304.9 7.4 multiply_reduce_fusion.2
  313.6 16.4 %fusion.9 = bf16[8,128,3072]{2,1,0:T(8,128)(2,1)} fusion(f32[8,128,3072]{2,1,0:T(8,128)} %copy-done.105, bf16[3072,768]{1,0:T(8,128)(2,1)} %param.41, f32[8,128,768]{2,1,0:T(8,128)S(1)} %subtract_multiply_fusion), kind=kOutput, calls=%fused_computation.13 | convolution fusion | flops 4895539200 | bytes 26738688 | tf_op jit(solution)/shard_map/...n,kn->...k/dot_general | solution.py:34
  330.1 8.5 multiply_reduce_fusion.3
  360.2 7.0 fusion.142
  374.5 7.1 bitcast_convert_fusion.3
  417.8 13.4 %fusion.100 = bf16[8,12,64,128]{3,2,1,0:T(8,128)(2,1)} fusion(bf16[8,128,12,64]{1,3,2,0:T(8,128)(2,1)} %bitcast.237, f32[8,12,128,128]{2,3,1,0:T(8,128)} %fusion.236, f32[8,12,128,128]{2,3,1,0:T(8,128)} %copy-done.1, f32[8,12,128]{2,1,0:T(8,128)} %log_add_fusion), kind=kOutput, calls=%fused_computation.124 | convolution fusion | flops 216281216 | bytes 15777792 | tf_op jit(solution)/shard_map/bhrs,brhd->bshd/dot_general | solution.py:81
  433.8 13.7 %fusion.97 = bf16[8,12,64,128]{3,2,1,0:T(8,128)(2,1)} fusion(bf16[8,128,12,64]{1,3,2,0:T(8,128)(2,1)} %bitcast.235, f32[8,12,128,128]{2,3,1,0:T(8,128)} %fusion.236, f32[8,12,128,128]{2,3,1,0:T(8,128)} %copy-done.1, f32[8,12,128]{2,1,0:T(8,128)} %log_add_fusion), kind=kOutput, calls=%fused_computation.123 | convolution fusion | flops 216281216 | bytes 15777792 | tf_op jit(solution)/shard_map/bhrs,bshd->brhd/dot_general | solution.py:80
  450.4 8.7 bitcast_convert_fusion.2
  459.2 12.6 %bitcast_convert_fusion = bf16[3072,768]{1,0:T(8,128)(2,1)} fusion(f32[8,128,768]{2,1,0:T(8,128)} %copy-done.14, f32[8,128,3072]{2,1,0:T(8,128)} %copy-done.105), kind=kOutput, calls=%fused_computation.15 | convolution fusion | flops 4863295488 | bytes 20447232 | tf_op jit(solution)/shard_map/dot_general | solution.py:40
  472.6 10.1 bitcast_convert_fusion.1
  490.6 53.4 %reduce-scatter.12.cloned.1.call-done = bf16[96,2304]{1,0:T(8,128)(2,1)} async-done(((bf16[768,2304]{1,0:T(8,128)(2,1)}), bf16[96,2304]{1,0:T(8,128)(2,1)}) %reduce-scatter.12.cloned.1.call-update) | async-done | bytes 442384 | tf_op jit(solution)/shard_map/reduce_scatter | solution.py:338
  544.0 72.0 %reduce-scatter.32.cloned.1.call-done = bf16[96,1536]{1,0:T(8,128)(2,1)} async-done(((bf16[768,1536]{1,0:T(8,128)(2,1)}), bf16[96,1536]{1,0:T(8,128)(2,1)}) %reduce-scatter.32.cloned.1.call-update) | async-done | bytes 294928 | tf_op jit(solution)/shard_map/reduce_scatter | solution.py:383
  616.0 98.1 %reduce-scatter.22.cloned.1.call-done = bf16[384,768]{1,0:T(8,128)(2,1)} async-done(((bf16[3072,768]{1,0:T(8,128)(2,1)}), bf16[384,768]{1,0:T(8,128)(2,1)}) %reduce-scatter.22.cloned.1.call-update) | async-done | bytes 589840 | tf_op jit(solution)/shard_map/reduce_scatter | solution.py:359
  714.1 98.8 %reduce-scatter.20.cloned.1.call-done = bf16[96,3072]{1,0:T(8,128)(2,1)} async-done(((bf16[768,3072]{1,0:T(8,128)(2,1)}), bf16[96,3072]{1,0:T(8,128)(2,1)}) %reduce-scatter.20.cloned.1.call-update) | async-done | bytes 589840 | tf_op jit(solution)/shard_map/reduce_scatter | solution.py:356
  812.9 82.6 %reduce-scatter.24.cloned.1.call-done = bf16[96,2304]{1,0:T(8,128)(2,1)} async-done(((bf16[768,2304]{1,0:T(8,128)(2,1)}), bf16[96,2304]{1,0:T(8,128)(2,1)}) %reduce-scatter.24.cloned.1.call-update) | async-done | bytes 442384 | tf_op jit(solution)/shard_map/reduce_scatter | solution.py:365
  895.5 98.5 %reduce-scatter.30.cloned.1.call-done = bf16[384,768]{1,0:T(8,128)(2,1)} async-done(((bf16[3072,768]{1,0:T(8,128)(2,1)}), bf16[384,768]{1,0:T(8,128)(2,1)}) %reduce-scatter.30.cloned.1.call-update) | async-done | bytes 589840 | tf_op jit(solution)/shard_map/reduce_scatter | solution.py:377
  994.0 98.9 %reduce-scatter.28.cloned.1.call-done = bf16[96,3072]{1,0:T(8,128)(2,1)} async-done(((bf16[768,3072]{1,0:T(8,128)(2,1)}), bf16[96,3072]{1,0:T(8,128)(2,1)}) %reduce-scatter.28.cloned.1.call-update) | async-done | bytes 589840 | tf_op jit(solution)/shard_map/reduce_scatter | solution.py:374
  1107.3 35.9 %all-reduce.6 = (bf16[768]{0:T(1024)(128)(2,1)}, bf16[768]{0:T(1024)(128)(2,1)S(1)}, bf16[768]{0:T(1024)(128)(2,1)}, bf16[768]{0:T(1024)(128)(2,1)}, bf16[768]{0:T(1024)(128)(2,1)}, /*index=5*/bf16[768]{0:T(1024)(128)(2,1)}) all-reduce(bf16[768]{0:T(1024)(128)(2,1)} %get-tuple-element.29, ...), channel_id=2, replica_groups=mesh['seq'=4,'nbr'=8] {'nbr'}, use_global_device_ids=true, to_apply=%region_27.28.clone | all-reduce | flops 4608 | bytes 18432
  1161.9 20.1 %all-reduce.11.cloned.1.call-done = (bf16[96,2304]{1,0:T(8,128)(2,1)}, bf16[96,768]{1,0:T(8,128)(2,1)}, bf16[96,768]{1,0:T(8,128)(2,1)}, bf16[96,768]{1,0:T(8,12...) async-done(((bf16[96,2304]{1,0:T(8,128)(2,1)}, ...) | async-done | bytes 4128784 | tf_op jit(solution)/shard_map/psum | solution.py:389
  (410 shorter events, 324.3 us)
Async XLA Ops:
  57.4 42.4 %all-to-all-start = ((bf16[8,128,1536]{2,1,0:T(8,128)(2,1)}), bf16[8,128,1536]{2,1,0:T(8,128)(2,1)}, u32[]{:S(2)}, u32[]{:S(2)}) async-start(bf16[8,128,1536]{2,1,0:T(8,128)(2,1)} %convolution_convert_fusion.5), calls=%async_computation | async-start | bytes 6291456 | tf_op jit(solution)/shard_map/all_to_all | solution.py:327
  62.2 428.5 %reduce-scatter.18.cloned.1.call-start = ((), (), s32[]{:S(2)}) async-start(), calls=%async_computation.16 | async-start | bytes 1327104 | tf_op jit(solution)/shard_map/reduce_scatter | solution.py:350
  124.9 9.5 copy-start.8
  137.3 353.4 %reduce-scatter.16.cloned.1.call-start = ((), (), s32[]{:S(2)}) async-start(), calls=%async_computation.15 | async-start | bytes 1327104 | tf_op jit(solution)/shard_map/reduce_scatter | solution.py:347
  263.3 41.7 %all-to-all-start.1 = ((bf16[8,128,1536]{2,1,0:T(8,128)(2,1)}), bf16[8,128,1536]{2,1,0:T(8,128)(2,1)}, u32[]{:S(2)}, u32[]{:S(2)}) async-start(bf16[8,128,1536]{2,1,0:T(8,128)(2,1)} %convert_element_type.376), calls=%async_computation.7 | async-start | bytes 6291456 | tf_op jit(solution)/shard_map/all_to_all | solution.py:331
  267.9 222.7 %reduce-scatter.14.cloned.1.call-start = ((), (), s32[]{:S(2)}) async-start(), calls=%async_computation.14 | async-start | bytes 1327104 | tf_op jit(solution)/shard_map/reduce_scatter | solution.py:341
  273.8 216.8 %reduce-scatter.26.cloned.1.call-start = ((), (), s32[]{:S(2)}) async-start(), calls=%async_computation.20 | async-start | bytes 1327104 | tf_op jit(solution)/shard_map/reduce_scatter | solution.py:368
  312.4 17.6 %slice-start.6 = ((s8[4718592]{0:T(1024)(128)(4,1)}), s8[524288]{0:T(1024)(128)(4,1)S(1)}, s32[]{:S(2)}) async-start(s8[4718592]{0:T(1024)(128)(4,1)} %bitcast.267), calls=%async_computation.31 | async-start | bytes 1048576
  313.6 25.0 %copy-start.14 = (f32[8,128,768]{2,1,0:T(8,128)}, f32[8,128,768]{2,1,0:T(8,128)S(1)}, u32[]{:S(2)}) copy-start(f32[8,128,768]{2,1,0:T(8,128)S(1)} %subtract_multiply_fusion) | copy-start | bytes 9437188
  313.6 16.4 %copy-start.4 = (f32[8,128,768]{2,1,0:T(8,128)S(1)}, f32[8,128,768]{2,1,0:T(8,128)}, u32[]{:S(2)}) copy-start(f32[8,128,768]{2,1,0:T(8,128)} %copy-done.3) | copy-start | bytes 9437188
  313.6 16.4 %copy-start.53 = (f32[8,128]{1,0:T(8,128)S(1)}, f32[8,128]{1,0:T(8,128)}, u32[]{:S(2)}) copy-start(f32[8,128]{1,0:T(8,128)} %copy-done.52) | copy-start | bytes 12292
  313.6 16.4 %copy-start.65 = (f32[8,128]{1,0:T(8,128)S(1)}, f32[8,128]{1,0:T(8,128)}, u32[]{:S(2)}) copy-start(f32[8,128]{1,0:T(8,128)} %copy-done.64) | copy-start | bytes 12292
  313.6 16.4 %copy-start.81 = (f32[768]{0:T(1024)S(1)}, f32[768]{0:T(1024)}, u32[]{:S(2)}) copy-start(f32[768]{0:T(1024)} %param.39) | copy-start | bytes 9220
  313.6 16.4 %slice-start.7 = ((s8[4718592]{0:T(1024)(128)(4,1)}), s8[4194304]{0:T(1024)(128)(4,1)S(1)}, s32[]{:S(2)}) async-start(s8[4718592]{0:T(1024)(128)(4,1)} %bitcast.267), calls=%async_computation.32 | async-start | bytes 8388608
  343.3 200.7 %reduce-scatter.12.cloned.1.call-start = ((), (), s32[]{:S(2)}) async-start(), calls=%async_computation.13 | async-start | bytes 3981312 | tf_op jit(solution)/shard_map/reduce_scatter | solution.py:338
  373.8 242.1 %reduce-scatter.32.cloned.1.call-start = ((), (), s32[]{:S(2)}) async-start(), calls=%async_computation.23 | async-start | bytes 2654208 | tf_op jit(solution)/shard_map/reduce_scatter | solution.py:383
  381.7 332.4 %reduce-scatter.22.cloned.1.call-start = ((), (), s32[]{:S(2)}) async-start(), calls=%async_computation.18 | async-start | bytes 5308416 | tf_op jit(solution)/shard_map/reduce_scatter | solution.py:359
  388.2 424.8 %reduce-scatter.20.cloned.1.call-start = ((), (), s32[]{:S(2)}) async-start(), calls=%async_computation.17 | async-start | bytes 5308416 | tf_op jit(solution)/shard_map/reduce_scatter | solution.py:356
  394.2 501.3 %reduce-scatter.24.cloned.1.call-start = ((), (), s32[]{:S(2)}) async-start(), calls=%async_computation.19 | async-start | bytes 3981312 | tf_op jit(solution)/shard_map/reduce_scatter | solution.py:365
  459.2 534.8 %reduce-scatter.30.cloned.1.call-start = ((), (), s32[]{:S(2)}) async-start(), calls=%async_computation.22 | async-start | bytes 5308416 | tf_op jit(solution)/shard_map/reduce_scatter | solution.py:377
  471.9 620.9 %reduce-scatter.28.cloned.1.call-start = ((), (), s32[]{:S(2)}) async-start(), calls=%async_computation.21 | async-start | bytes 5308416 | tf_op jit(solution)/shard_map/reduce_scatter | solution.py:374
  482.7 699.3 %all-reduce.11.cloned.1.call-start = ((), (), s32[]{:S(2)}) async-start(), calls=%async_computation.24 | async-start | bytes 8257536 | tf_op jit(solution)/shard_map/psum | solution.py:389
  1182.0 9.6 copy-start.40
  1182.0 10.6 copy-start.39
  (106 other events, 370.3 us)
Sparse Core Ops, SparseCore 0:
  137.4 65.1 reduce-scatter.17
  263.4 65.1 reduce-scatter.15
  332.6 62.9 reduce-scatter.13
  399.4 62.9 reduce-scatter.25
  465.9 78.0 reduce-scatter.11
  547.3 68.5 reduce-scatter.31
  619.6 94.4 reduce-scatter.21
  717.7 95.1 reduce-scatter.19
  816.6 78.8 reduce-scatter.23
  899.0 94.9 reduce-scatter.29
  997.6 95.1 reduce-scatter.27
  1095.8 86.1 all-reduce.10
where the time goes:
time: 1210 us; the launch traced here: 1200 us
  waiting for transfers between devices  658 us (54%)
  matrix products  291 us (24%)
  local copies, waits for them, and re-layouts  125 us (10%)
  other arithmetic  59.1 us (5%)
  blocking collectives  42.7 us (4%)
  between operations  17.1 us (1%)
    reduce_scatter x1, waiting for transfers between devices, body(): lax.psum_scatter(local[13].astype(jnp.bfloat16), 'nbr', scatter_dimension...  98.9 us
    reduce_scatter x1, waiting for transfers between devices, body(): lax.psum_scatter(local[7].astype(jnp.bfloat16), 'nbr', scatter_dimension=...  98.8 us
    reduce_scatter x1, waiting for transfers between devices, body(): lax.psum_scatter(local[14].astype(jnp.bfloat16), 'nbr', scatter_dimension...  98.5 us
    reduce_scatter x1, waiting for transfers between devices, body(): lax.psum_scatter(local[8].astype(jnp.bfloat16), 'nbr', scatter_dimension=...  98.1 us
    reduce_scatter x1, waiting for transfers between devices, body(): lax.psum_scatter(local[10].astype(jnp.bfloat16), 'nbr', scatter_dimension...  82.6 us
    reduce_scatter x1, waiting for transfers between devices, body(): lax.psum_scatter(local[16].astype(jnp.bfloat16), 'nbr', scatter_dimension...  72 us
    dot_general x11, matrix products, weight_grad(): lax.dot_general(flat_values, flat_grad, (((0,), (0,)), ((), ())), preferr...  61.9 us
    dot_general x11, matrix products, times_back(): jnp.einsum('...n,kn->...k', grad, weight, preferred_element_type=jnp.floa...  60.3 us
  transfers between devices with their start and end apart: 14, of which 10 were waited for; matrix products, arithmetic and copies ran while one was open for 30% of the time, Pallas kernels for 0%

commit v1 on v0

v1 whole, which is shorter than its diff:
```python
from functools import partial

import jax
import jax.numpy as jnp
from jax import lax
from jax.experimental import pallas as pl
from jax.experimental.pallas import tpu as pltpu
from jax.sharding import PartitionSpec as P

D = 768
HEADS = 12
HD = 64
CH = 64
PAIRS = HEADS // 2
LANES = 2 * HD
SCALE = HD ** (-0.5)
F32 = jnp.float32
BF16 = jnp.bfloat16


def norm_forward(values, gain):
    centred = values - jnp.mean(values, axis=-1, keepdims=True)
    inverse = lax.rsqrt(jnp.mean(centred * centred, axis=-1, keepdims=True) + 1e-05)
    normed = centred * inverse
    return ((normed * gain).astype(BF16), normed, inverse)


def norm_backward(grad, normed, inverse, gain):
    scaled = grad * gain
    inner = jnp.mean(scaled * normed, axis=-1, keepdims=True)
    return inverse * (scaled - jnp.mean(scaled, axis=-1, keepdims=True) - normed * inner)


def times(values, weight):
    return lax.dot_general(values, weight, (((1,), (0,)), ((), ())), preferred_element_type=F32)


def times_back(grad, weight):
    return lax.dot_general(grad, weight, (((1,), (1,)), ((), ())), preferred_element_type=F32)


def weight_grad(values, grad):
    return lax.dot_general(values, grad, (((0,), (0,)), ((), ())), preferred_element_type=F32)


def curve_grad(rising, upstream):
    return jax.vjp(partial(jax.nn.gelu, approximate=True), rising)[1](upstream)[0]


def dot_nt(a, b):
    return lax.dot_general(a, b, (((1,), (1,)), ((), ())), preferred_element_type=F32)


def dot_nn(a, b):
    return lax.dot_general(a, b, (((1,), (0,)), ((), ())), preferred_element_type=F32)


def dot_tn(a, b):
    return lax.dot_general(a, b, (((0,), (0,)), ((), ())), preferred_element_type=F32)


def stack_pair(block):
    lane = lax.broadcasted_iota(jnp.int32, block.shape, 1)
    zero = jnp.zeros_like(block)
    return jnp.concatenate([jnp.where(lane < HD, block, zero), jnp.where(lane >= HD, block, zero)], axis=0)


def unstack_pair(stacked):
    half = stacked.shape[0] // 2
    lane = lax.broadcasted_iota(jnp.int32, (half, LANES), 1)
    return jnp.where(lane < HD, stacked[:half], stacked[half:])


def softmax_halves(products, allowed):
    width = products.shape[1] // 2
    parts = []
    for h in range(2):
        scores = products[:, h * width : (h + 1) * width] * SCALE
        if allowed is not None:
            scores = jnp.where(allowed, scores, -1000000000.0)
        exponent = jnp.exp(scores - jnp.max(scores, axis=-1, keepdims=True))
        parts.append(exponent * (1.0 / jnp.sum(exponent, axis=-1, keepdims=True)))
    return parts


def pair_forward(queries, keys, values, allowed):
    probs = softmax_halves(dot_nt(queries, stack_pair(keys)), allowed)
    probs = jnp.concatenate([p.astype(BF16) for p in probs], axis=1)
    return dot_nn(probs, stack_pair(values)).astype(BF16)


def pair_backward(queries, keys, values, outgoing, allowed):
    keys2 = stack_pair(keys)
    probs = softmax_halves(dot_nt(queries, keys2), allowed)
    rounded = jnp.concatenate([p.astype(BF16) for p in probs], axis=1)
    value_grad = unstack_pair(dot_tn(rounded, outgoing))
    prob_grad = dot_nt(outgoing, stack_pair(values))
    width = prob_grad.shape[1] // 2
    parts = []
    for h in range(2):
        part = prob_grad[:, h * width : (h + 1) * width]
        inner = jnp.sum(probs[h] * part, axis=-1, keepdims=True)
        parts.append((probs[h] * (part - inner) * SCALE).astype(BF16))
    score_grad = jnp.concatenate(parts, axis=1)
    query_grad = dot_nn(score_grad, keys2)
    key_grad = unstack_pair(dot_tn(score_grad, queries))
    return query_grad.astype(BF16), key_grad.astype(BF16), value_grad.astype(BF16)


def col(pair, third=0):
    return slice(third * D + pair * LANES, third * D + (pair + 1) * LANES)


def estimate(flops, nbytes, exps=0):
    return pl.CostEstimate(flops=int(flops), bytes_accessed=int(nbytes), transcendentals=int(exps))


def enc_attend_kernel(joint_ref, mixed_ref):
    for p in range(PAIRS):
        mixed_ref[0, :, col(p)] = pair_forward(
            joint_ref[0, :, col(p, 0)], joint_ref[0, :, col(p, 1)], joint_ref[0, :, col(p, 2)], None
        )


def enc_attend(joint):
    count, rows, _ = joint.shape
    return pl.pallas_call(
        enc_attend_kernel,
        grid=(count,),
        in_specs=[pl.BlockSpec((1, rows, 3 * D), lambda i: (i, 0, 0))],
        out_specs=pl.BlockSpec((1, rows, D), lambda i: (i, 0, 0)),
        out_shape=jax.ShapeDtypeStruct((count, rows, D), BF16),
        cost_estimate=estimate(4 * count * rows * rows * D * 4, count * rows * D * 8, count * rows * rows * HEADS),
        name="enc_attend",
    )(joint)


def enc_attend_back_kernel(joint_ref, grad_ref, out_ref):
    for p in range(PAIRS):
        grads = pair_backward(
            joint_ref[0, :, col(p, 0)], joint_ref[0, :, col(p, 1)], joint_ref[0, :, col(p, 2)], grad_ref[0, :, col(p)], None
        )
        for third in range(3):
            out_ref[0, :, col(p, third)] = grads[third]


def enc_attend_back(joint, grad):
    count, rows, _ = joint.shape
    return pl.pallas_call(
        enc_attend_back_kernel,
        grid=(count,),
        in_specs=[
            pl.BlockSpec((1, rows, 3 * D), lambda i: (i, 0, 0)),
            pl.BlockSpec((1, rows, D), lambda i: (i, 0, 0)),
        ],
        out_specs=pl.BlockSpec((1, rows, 3 * D), lambda i: (i, 0, 0)),
        out_shape=jax.ShapeDtypeStruct((count, rows, 3 * D), BF16),
        cost_estimate=estimate(10 * count * rows * rows * D * 4, count * rows * D * 14, count * rows * rows * HEADS),
        name="enc_attend_back",
    )(joint, grad)


def causal_mask(rows, length):
    row = lax.broadcasted_iota(jnp.int32, (rows, rows), 0)
    column = lax.broadcasted_iota(jnp.int32, (rows, rows), 1)
    return (column <= row) & (column < length)


def self_attend_kernel(length_ref, q_ref, k_ref, v_ref, out_ref):
    allowed = causal_mask(q_ref.shape[0], length_ref[0])
    out_ref[...] = pair_forward(q_ref[...], k_ref[...], v_ref[...], allowed)


def self_attend(joint, lengths):
    rows = joint.shape[0]
    return pl.pallas_call(
        self_attend_kernel,
        grid_spec=pltpu.PrefetchScalarGridSpec(
            num_scalar_prefetch=1,
            grid=(PAIRS,),
            in_specs=[pl.BlockSpec((rows, LANES), lambda p, _, t=t: (0, t * PAIRS + p)) for t in range(3)],
            out_specs=pl.BlockSpec((rows, LANES), lambda p, _: (0, p)),
        ),
        out_shape=jax.ShapeDtypeStruct((rows, D), BF16),
        cost_estimate=estimate(4 * rows * rows * D * 4, rows * D * 8, rows * rows * HEADS),
        name="self_attend",
    )(lengths, joint, joint, joint)


def self_attend_back_kernel(length_ref, q_ref, k_ref, v_ref, grad_ref, dq_ref, dk_ref, dv_ref):
    allowed = causal_mask(q_ref.shape[0], length_ref[0])
    grads = pair_backward(q_ref[...], k_ref[...], v_ref[...], grad_ref[...], allowed)
    dq_ref[...] = grads[0]
    dk_ref[...] = grads[1]
    dv_ref[...] = grads[2]


def self_attend_back(joint, grad, lengths):
    rows = joint.shape[0]
    block = pl.BlockSpec((rows, LANES), lambda p, _: (0, p))
    return pl.pallas_call(
        self_attend_back_kernel,
        grid_spec=pltpu.PrefetchScalarGridSpec(
            num_scalar_prefetch=1,
            grid=(PAIRS,),
            in_specs=[pl.BlockSpec((rows, LANES), lambda p, _, t=t: (0, t * PAIRS + p)) for t in range(3)] + [block],
            out_specs=[block] * 3,
        ),
        out_shape=[jax.ShapeDtypeStruct((rows, D), BF16)] * 3,
        cost_estimate=estimate(10 * rows * rows * D * 4, rows * D * 14, rows * rows * HEADS),
        name="self_attend_back",
    )(lengths, joint, joint, joint, grad)


def cross_attend_kernel(order_ref, asked_ref, first_ref, second_ref, out_ref):
    for p in range(PAIRS):
        keys = jnp.concatenate([first_ref[0, :, col(p, 0)], second_ref[0, :, col(p, 0)]], axis=0)
        values = jnp.concatenate([first_ref[0, :, col(p, 1)], second_ref[0, :, col(p, 1)]], axis=0)
        out_ref[:, col(p)] = pair_forward(asked_ref[:, col(p)], keys, values, None)


def cross_attend(asked, memory, order):
    rows = asked.shape[0]
    count, places, _ = memory.shape
    return pl.pallas_call(
        cross_attend_kernel,
        grid_spec=pltpu.PrefetchScalarGridSpec(
            num_scalar_prefetch=1,
            grid=(rows // CH,),
            in_specs=[
                pl.BlockSpec((CH, D), lambda c, order: (c, 0)),
                pl.BlockSpec((1, places, 2 * D), lambda c, order: (order[2 * c], 0, 0)),
                pl.BlockSpec((1, places, 2 * D), lambda c, order: (order[2 * c + 1], 0, 0)),
            ],
            out_specs=pl.BlockSpec((CH, D), lambda c, order: (c, 0)),
        ),
        out_shape=jax.ShapeDtypeStruct((rows, D), BF16),
        cost_estimate=estimate(4 * rows * 2 * places * D * 4, rows * D * 4 + count * places * D * 4, rows * 2 * places * HEADS),
        name="cross_attend",
    )(order, asked, memory, memory)


def cross_attend_back_kernel(order_ref, asked_ref, first_ref, second_ref, grad_ref, dq_ref, dmem_ref):
    c = pl.program_id(0)
    first, second = order_ref[2 * c], order_ref[2 * c + 1]
    places = first_ref.shape[1]
    for p in range(PAIRS):
        keys = jnp.concatenate([first_ref[0, :, col(p, 0)], second_ref[0, :, col(p, 0)]], axis=0)
        values = jnp.concatenate([first_ref[0, :, col(p, 1)], second_ref[0, :, col(p, 1)]], axis=0)
        dq, dk, dv = pair_backward(asked_ref[:, col(p)], keys, values, grad_ref[:, col(p)], None)
        dq_ref[:, col(p)] = dq
        dmem_ref[first, :, col(p, 0)] = dk[:places]
        dmem_ref[second, :, col(p, 0)] = dk[places:]
        dmem_ref[first, :, col(p, 1)] = dv[:places]
        dmem_ref[second, :, col(p, 1)] = dv[places:]


def cross_attend_back(asked, memory, grad, order):
    rows = asked.shape[0]
    count, places, _ = memory.shape
    return pl.pallas_call(
        cross_attend_back_kernel,
        grid_spec=pltpu.PrefetchScalarGridSpec(
            num_scalar_prefetch=1,
            grid=(rows // CH,),
            in_specs=[
                pl.BlockSpec((CH, D), lambda c, order: (c, 0)),
                pl.BlockSpec((1, places, 2 * D), lambda c, order: (order[2 * c], 0, 0)),
                pl.BlockSpec((1, places, 2 * D), lambda c, order: (order[2 * c + 1], 0, 0)),
                pl.BlockSpec((CH, D), lambda c, order: (c, 0)),
            ],
            out_specs=[
                pl.BlockSpec((CH, D), lambda c, order: (c, 0)),
                pl.BlockSpec((count, places, 2 * D), lambda c, order: (0, 0, 0)),
            ],
        ),
        out_shape=[jax.ShapeDtypeStruct((rows, D), BF16), jax.ShapeDtypeStruct(memory.shape, BF16)],
        cost_estimate=estimate(10 * rows * 2 * places * D * 4, rows * D * 6 + count * places * D * 8, rows * 2 * places * HEADS),
        name="cross_attend_back",
    )(order, asked, memory, memory, grad)


def swap(value, axis, size, mask):
    return lax.ppermute(value, axis, [(i, i ^ mask) for i in range(size)])


def bit_of(axis, mask):
    return (lax.axis_index(axis) // mask) % 2


def pick(value, dim, index):
    return lax.dynamic_index_in_dim(value, index, dim, keepdims=False)


def halve(value, dim, axis, size, mask):
    bit = bit_of(axis, mask)
    arrived = swap(pick(value, dim, 1 - bit), axis, size, mask)
    return (pick(value, dim, bit).astype(F32) + arrived.astype(F32)).astype(BF16)


def join(value, dim, axis, size, mask):
    arrived = swap(value, axis, size, mask)
    bit = bit_of(axis, mask)
    return jnp.where(
        bit == 0, jnp.concatenate([value, arrived], axis=dim), jnp.concatenate([arrived, value], axis=dim)
    )


def masks(size):
    found, mask = [], 1
    while mask < size:
        found.append(mask)
        mask *= 2
    return found


def reduce_group(pairs, sizes, rows_first):
    nseq, nnbr = sizes
    core = bit_of("seq", 1)
    parts = []
    for values, grad in pairs:
        half = grad.shape[1] // 2
        theirs = lax.dynamic_slice_in_dim(grad, (1 - core) * half, half, 1)
        ours = lax.dynamic_slice_in_dim(grad, core * half, half, 1)
        arrived = swap(weight_grad(values, theirs).astype(BF16), "seq", nseq, 1)
        parts.append((weight_grad(values, ours) + arrived.astype(F32)).astype(BF16))
    widths = [part.shape[1] for part in parts]
    total = parts[0] if len(parts) == 1 else jnp.concatenate(parts, axis=1)
    bits = masks(nnbr)
    rows = total.shape[0] // nnbr
    total = total.reshape((2,) * len(bits) + (rows, total.shape[1]))
    seq_bits = masks(nseq)[1:]

    def over_seq(total):
        for mask in seq_bits:
            shape = total.shape
            total = total.reshape(shape[:-2] + (2, shape[-2] // 2, shape[-1]))
            total = halve(total, total.ndim - 3, "seq", nseq, mask)
        return total

    def over_nbr(total):
        left = list(reversed(bits))
        for mask in bits:
            total = halve(total, left.index(mask), "nbr", nnbr, mask)
            left.remove(mask)
        return total

    if rows_first:
        total = over_nbr(over_seq(total))
        for mask in reversed(seq_bits):
            total = join(total, 0, "seq", nseq, mask)
    else:
        total = over_nbr(total)
        for mask in seq_bits:
            total = (total.astype(F32) + swap(total, "seq", nseq, mask).astype(F32)).astype(BF16)
    other = swap(total, "seq", nseq, 1)
    results, start = [], 0
    for width in widths:
        mine, theirs = total[:, start : start + width], other[:, start : start + width]
        results.append(
            jnp.where(
                core == 0, jnp.concatenate([mine, theirs], axis=1), jnp.concatenate([theirs, mine], axis=1)
            ).astype(F32)
        )
        start += width
    return results


def gain_grad(gain, weight, grad, nnbr):
    rows = weight.shape[0] // nnbr
    start = lax.axis_index("nbr") * rows
    own = lax.dynamic_slice_in_dim(weight, start, rows, 0).astype(F32)
    return jnp.sum(own * grad, axis=1) / lax.dynamic_slice_in_dim(gain, start, rows, 0)


def body(
    sizes,
    tokens,
    neighbours,
    out_grad,
    lengths,
    slot_order,
    selfgain,
    selfjoint,
    selfmerge,
    crossgain,
    crossquery,
    crossmerge,
    feedgain,
    feedup,
    feeddown,
    codergain,
    coderjoint,
    codermerge,
    codermid,
    coderup,
    coderdown,
    codertop,
    memorymap,
):
    nseq, nnbr = sizes
    me = lax.axis_index("seq")
    count, places, _ = neighbours.shape
    cap = count // nseq
    flat = count * places

    ordered = jnp.concatenate(
        [lax.dynamic_slice_in_dim(neighbours, (me ^ m) * cap, cap, 0) for m in range(nseq)], axis=0
    )
    embedded = ordered.reshape(flat, D).astype(F32)
    enc_normed, _, _ = norm_forward(embedded, codergain)
    enc_joint = times(enc_normed, coderjoint).astype(BF16).reshape(count, places, 3 * D)
    enc_mixed = enc_attend(enc_joint).reshape(flat, D)
    enc_middle = embedded + times(enc_mixed, codermerge)
    enc_normed_b, enc_plain_b, enc_inverse_b = norm_forward(enc_middle, codermid)
    enc_rising = times(enc_normed_b, coderup)
    enc_hidden = jax.nn.gelu(enc_rising, approximate=True).astype(BF16)
    enc_upper = enc_middle + times(enc_hidden, coderdown)
    enc_normed_c, enc_plain_c, enc_inverse_c = norm_forward(enc_upper, codertop)
    blocks = enc_normed_c.reshape(nseq, cap * places, D)
    received = jnp.concatenate(
        [blocks[m] if m == 0 else swap(blocks[m], "seq", nseq, m) for m in range(nseq)], axis=0
    )

    sequence = tokens[0].astype(F32)
    rows = sequence.shape[0]
    normed_a, plain_a, inverse_a = norm_forward(sequence, selfgain)
    joint = times(normed_a, selfjoint).astype(BF16)
    mixed = self_attend(joint, lengths)
    after_self = sequence + times(mixed, selfmerge)
    normed_b, plain_b, inverse_b = norm_forward(after_self, crossgain)
    asked = times(normed_b, crossquery).astype(BF16)

    memory = times(received, memorymap).astype(BF16).reshape(count, places, 2 * D)
    order = slot_order[0]
    order = ((order // cap) ^ me) * cap + order % cap
    crossed = cross_attend(asked, memory, order)
    live = (jnp.arange(rows, dtype=jnp.int32) // CH * CH < lengths[0]).astype(F32)[:, None]
    after_cross = after_self + times(crossed, crossmerge) * live
    normed_c, plain_c, inverse_c = norm_forward(after_cross, feedgain)
    rising = times(normed_c, feedup)
    hidden = jax.nn.gelu(rising, approximate=True).astype(BF16)
    output = (after_cross + times(hidden, feeddown)).astype(BF16)[None]

    down_in = out_grad[0]
    (grad_feeddown,) = reduce_group([(hidden, down_in)], sizes, False)
    rising_grad = curve_grad(rising, times_back(down_in, feeddown)).astype(BF16)
    (grad_feedup,) = reduce_group([(normed_c, rising_grad)], sizes, True)
    cross_total = down_in.astype(F32) + norm_backward(times_back(rising_grad, feedup), plain_c, inverse_c, feedgain)
    cross_in = (cross_total * live).astype(BF16)
    crossed_grad = times_back(cross_in, crossmerge).astype(BF16)
    asked_grad, memory_grad = cross_attend_back(asked, memory, crossed_grad, order)
    memory_grad = memory_grad.reshape(flat, 2 * D)
    back = times_back(memory_grad, memorymap).astype(BF16).reshape(nseq, cap * places, D)
    returned = jnp.concatenate(
        [back[m] if m == 0 else swap(back[m], "seq", nseq, m) for m in range(nseq)], axis=0
    ).astype(F32)
    grad_crossmerge, grad_crossquery, grad_memorymap = reduce_group(
        [(crossed, cross_in), (normed_b, asked_grad), (received, memory_grad)], sizes, False
    )
    self_total = cross_total + norm_backward(times_back(asked_grad, crossquery), plain_b, inverse_b, crossgain)
    self_in = self_total.astype(BF16)
    mixed_grad = times_back(self_in, selfmerge).astype(BF16)
    joint_grad = jnp.concatenate(self_attend_back(joint, mixed_grad, lengths), axis=1)
    grad_selfmerge, grad_selfjoint = reduce_group([(mixed, self_in), (normed_a, joint_grad)], sizes, False)
    input_grad = (self_total + norm_backward(times_back(joint_grad, selfjoint), plain_a, inverse_a, selfgain))[None]

    upper_total = norm_backward(returned, enc_plain_c, enc_inverse_c, codertop)
    enc_down_in = upper_total.astype(BF16)
    (grad_coderdown,) = reduce_group([(enc_hidden, enc_down_in)], sizes, True)
    enc_rising_grad = curve_grad(enc_rising, times_back(enc_down_in, coderdown)).astype(BF16)
    (grad_coderup,) = reduce_group([(enc_normed_b, enc_rising_grad)], sizes, False)
    middle_total = upper_total + norm_backward(
        times_back(enc_rising_grad, coderup), enc_plain_b, enc_inverse_b, codermid
    )
    enc_merge_in = middle_total.astype(BF16)
    enc_mixed_grad = times_back(enc_merge_in, codermerge).astype(BF16).reshape(count, places, D)
    enc_joint_grad = enc_attend_back(enc_joint, enc_mixed_grad).reshape(flat, 3 * D)
    grad_codermerge, grad_coderjoint = reduce_group(
        [(enc_mixed, enc_merge_in), (enc_normed, enc_joint_grad)], sizes, True
    )
    return (
        output,
        input_grad,
        gain_grad(selfgain, selfjoint, grad_selfjoint, nnbr),
        grad_selfjoint,
        grad_selfmerge,
        gain_grad(crossgain, crossquery, grad_crossquery, nnbr),
        grad_crossquery,
        grad_crossmerge,
        gain_grad(feedgain, feedup, grad_feedup, nnbr),
        grad_feedup,
        grad_feeddown,
        gain_grad(codergain, coderjoint, grad_coderjoint, nnbr),
        grad_coderjoint,
        grad_codermerge,
        gain_grad(codermid, coderup, grad_coderup, nnbr),
        grad_coderup,
        grad_coderdown,
        gain_grad(codertop, memorymap, grad_memorymap, nnbr),
        grad_memorymap,
    )


def solution(mesh):
    spread = ("seq", "nbr")
    sizes = (mesh.shape["seq"], mesh.shape["nbr"])
    placed = (
        P(spread, None, None),
        P(spread, None, None),
        P(spread, None, None),
        P(spread),
        P(spread, None),
    ) + (P(),) * 17
    gain, weight = P("nbr"), P("nbr", None)
    return jax.shard_map(
        partial(body, sizes),
        mesh=mesh,
        in_specs=placed,
        out_specs=(
            P(spread, None, None),
            P(spread, None, None),
            gain,
            weight,
            weight,
            gain,
            weight,
            weight,
            gain,
            weight,
            weight,
            gain,
            weight,
            weight,
            gain,
            weight,
            weight,
            gain,
            weight,
        ),
        check_vma=False,
    )
```

time: 1210 us -> 533 us (0.44)
  waiting for transfers between devices: 658 us -> 149 us
  matrix products: 291 us -> 166 us
  local copies, waits for them, and re-layouts: 125 us -> 25.5 us
  Pallas kernels: 0 us -> 80.8 us
  blocking collectives: 42.7 us -> 0 us
  starting transfers between devices: 10.8 us -> 51 us
  between operations: 17.1 us -> 3.9 us
    reduce_scatter x11 -> x0, waiting for transfers between devices: 602 us -> none  [the longest x1 98.9 us: body(): lax.psum_scatter(local[13].astype(jnp.bfloat16), 'nbr', scatter_dimension...]
    ppermute x0 -> x55, waiting for transfers between devices: none -> 149 us  [swap(): return lax.ppermute(value, axis, [(i, i ^ mask) for i in range(size)])]
    dot_general x51 -> x43, matrix products: 291 us -> 166 us  [the longest x22 68.9 us: weight_grad(): lax.dot_general(values, grad, (((0,), (0,)), ((), ())), preferred_element...]
    pallas_call x0 -> x6, Pallas kernels: none -> 80.8 us  [the longest x1 26.6 us: enc_attend_back(): pl.pallas_call(enc_attend_back_kernel, grid=(count,), in_specs=[pl.BlockS...]
    ppermute x0 -> x55, starting transfers between devices: none -> 51 us  [swap(): return lax.ppermute(value, axis, [(i, i ^ mask) for i in range(size)])]
    unnamed x1 -> x0, blocking collectives: 35.9 us -> none
    all_to_all x2 -> x0, waiting for transfers between devices: 35.8 us -> none  [the longest x1 31 us: body(): lax.all_to_all(memory_grad, 'seq', split_axis=0, concat_axis=0, tiled=True)]
    slice x11 -> x14, local copies, waits for them, and re-layouts: 26 us -> 1.47 us  [the longest x1 1.18 us: body(): blocks[m]]
  transfers between devices with their start and end apart: 14 -> 55, of which waited for: 10 -> 18; matrix products, arithmetic and copies ran while one was open for 30% -> 29% of each run, Pallas kernels for 0% -> 6%
where the time goes in v1:
time: 533 us; the launch traced here: 524 us
  matrix products  166 us (31%)
  waiting for transfers between devices  149 us (28%)
  Pallas kernels  80.8 us (15%)
  starting transfers between devices  51 us (10%)
  other arithmetic  47.9 us (9%)
  local copies, waits for them, and re-layouts  25.5 us (5%)
    ppermute x55, waiting for transfers between devices, swap(): return lax.ppermute(value, axis, [(i, i ^ mask) for i in range(size)])  149 us
    dot_general x22, matrix products, weight_grad(): lax.dot_general(values, grad, (((0,), (0,)), ((), ())), preferred_element...  68.9 us
    dot_general x11, matrix products, times(): lax.dot_general(values, weight, (((1,), (0,)), ((), ())), preferred_eleme...  52.6 us
    ppermute x55, starting transfers between devices, swap(): return lax.ppermute(value, axis, [(i, i ^ mask) for i in range(size)])  51 us
    dot_general x10, matrix products, times_back(): lax.dot_general(grad, weight, (((1,), (1,)), ((), ())), preferred_element...  44.7 us
    pallas_call x1, Pallas kernels, enc_attend_back(): pl.pallas_call(enc_attend_back_kernel, grid=(count,), in_specs=[pl.BlockS...  26.6 us
    pallas_call x1, Pallas kernels, cross_attend_back(): pl.pallas_call(cross_attend_back_kernel, grid_spec=pltpu.PrefetchScalarGr...  18.6 us
    reduce_sum x6, other arithmetic, gain_grad(): jnp.sum(own * grad, axis=1) / lax.dynamic_slice_in_dim(gain, start, rows, 0)  13.1 us
  transfers between devices with their start and end apart: 55, of which 18 were waited for; matrix products, arithmetic and copies ran while one was open for 29% of the time, Pallas kernels for 6%

profile of v1, /device:TPU:0, one launch (start us, length us, event | category | flops | bytes accessed | tf_op | source)
XLA Modules:
  0.0 524.0 jit_solution(18122496953780127425)
XLA Ops:
  11.5 5.6 %convolution_convert_fusion = bf16[1024,2304]{1,0:T(8,128)(2,1)} fusion(bf16[1024,768]{0,1:T(8,128)(2,1)S(1)} %multiply_convert_fusion.4, bf16[768,2304]{1,0:T(8,128)(2,1)S(1)} %copy-done.49), kind=kOutput, calls=%fused_computation.10 | convolution fusion | flops 3626237952 | bytes 9830400 | tf_op jit(solution)/shard_map/dot_general | solution.py:35
  17.2 10.4 %enc_attend.1 = bf16[8,128,768]{2,1,0:T(8,128)(2,1)} custom-call(bf16[8,128,2304]{2,1,0:T(8,128)(2,1)} %bitcast.287), custom_call_target="tpu_custom_call" | custom-call | flops 1610612736 | bytes 6291456 | tf_op jit(solution)/shard_map/enc_attend/pallas_call | solution.py:127
  33.3 11.8 %multiply_convert_fusion = (bf16[1024,3072]{1,0:T(8,128)(2,1)}, f32[1024,3072]{1,0:T(8,128)}) fusion(bf16[1024,768]{0,1:T(8,128)(2,1)S(1)} %multiply_convert_fusion.3, bf16[768,3072]{1,0:T(8,128)(2,1)S(1)} %bitcast.301), kind=kOutput, calls=%fused_computation.9 | convolution fusion | flops 4860149760 | bytes 25165824 | tf_op jit(solution)/shard_map/dot_general | solution.py:35
  45.1 7.7 %fusion.177 = (f32[1024]{0:T(1024)S(1)}, f32[1024,768]{0,1:T(8,128)S(1)}) fusion(f32[1024,768]{0,1:T(8,128)S(1)} %get-tuple-element.88, bf16[1024,3072]{1,0:T(8,128)(2,1)} %get-tuple-element.89, bf16[3072,768]{1,0:T(8,128)(2,1)S(1)} %bitcast.305), kind=kOutput, calls=%fused_computation.354 | convolution fusion | flops 4833410048 | bytes 17305600 | tf_op jit(solution)/shard_map/dot_general | solution.py:35
  64.6 5.8 %self_attend.1 = bf16[256,768]{1,0:T(8,128)(2,1)} custom-call(s32[1]{0:T(128)} %copy.131.length_ref, bf16[256,2304]{1,0:T(8,128)(2,1)} %convolution_convert_fusion.3.q_ref.k_ref.v_ref, bf16[256,2304]{1,0:T(8,128)(2,1)} %convolution_convert_fusion.3.q_ref.k_ref.v_ref, bf16[256,2304]{1,0:T(8,128)(2,1)} %convolution_convert_fusion.3.q_ref.k_ref.v_ref), custom_call_target="tpu_custom_call" | custom-call | flops 805306368 | bytes 1572864 | tf_op jit(solution)/shard_map/self_attend/pallas_call | solution.py:176
  76.6 6.4 %convolution_convert_fusion.4 = bf16[1024,1536]{1,0:T(8,128)(2,1)} fusion(bf16[768,1536]{1,0:T(8,128)(2,1)} %param.43, bf16[256,768]{0,1:T(8,128)(2,1)} %collective-permute-done.2, bf16[256,768]{0,1:T(8,128)(2,1)} %collective-permute-done.1, bf16[256,768]{0,1:T(8,128)(2,1)} %collective-permute-done, bf16[256,768]{0,1:T(8,128)(2,1)S(1)} %copy-done.42), kind=kOutput, calls=%fused_computation.20 | convolution fusion | flops 2423783424 | bytes 7077888 | tf_op jit(solution)/shard_map/dot_general | solution.py:35
  83.0 11.4 %cross_attend.1 = bf16[256,768]{1,0:T(8,128)(2,1)} custom-call(s32[8]{0:T(128)} %fusion.155.order_ref, bf16[256,768]{1,0:T(8,128)(2,1)} %convolution_convert_fusion.17.asked_ref, bf16[8,128,1536]{2,1,0:T(8,128)(2,1)} %bitcast.274, bf16[8,128,1536]{2,1,0:T(8,128)(2,1)} %bitcast.275), custom_call_target="tpu_custom_call" | custom-call | flops 805306368 | bytes 3932160 | tf_op jit(solution)/shard_map/cross_attend/pallas_call | solution.py:225
  111.2 18.6 %cross_attend_back.1 = (bf16[256,768]{1,0:T(8,128)(2,1)}, bf16[8,128,1536]{2,1,0:T(8,128)(2,1)}) custom-call(s32[8]{0:T(128)} %fusion.155.order_ref, bf16[256,768]{1,0:T(8,128)(2,1)} %convolution_convert_fusion.17.asked_ref, bf16[8,128,1536]{2,1,0:T(8,128)(2,1)} %bitcast.276, bf16[8,128,1536]{2,1,0:T(8,128)(2,1)} %bitcast.277, ...), custom_call_target="tpu_custom_call" | custom-call | flops 2013265920 | bytes 7471104 | tf_op jit(solution)/shard_map/cross_attend_back/pallas_call | solution.py:261
  139.0 7.9 %self_attend_back.1 = (bf16[256,768]{1,0:T(8,128)(2,1)}, bf16[256,768]{1,0:T(8,128)(2,1)}, bf16[256,768]{1,0:T(8,128)(2,1)}) custom-call(s32[1]{0:T(128)} %copy.131.length_ref, bf16[256,2304]{1,0:T(8,128)(2,1)} %convolution_convert_fusion.3.q_ref.k_ref.v_ref, bf16[256,2304]{1,0:T(8,128)(2,1)} %convolution_convert_fusion.3.q_ref.k_ref.v_ref, ...), custom_call_target="tpu_custom_call" | custom-call | flops 2013265920 | bytes 2752512 | tf_op jit(solution)/shard_map/self_attend_back/pallas_call | solution.py:201
  173.6 8.1 %collective-permute-done.32 = bf16[256,768]{0,1:T(8,128)(2,1)S(1)} collective-permute-done((bf16[256,768]{0,1:T(8,128)(2,1)S(1)}, bf16[256,768]{0,1:T(8,128)(2,1)S(1)}, u32[]{:S(2)}, u32[]{:S(2)}) %collective-permute-start.32) | collective-permute-done | bytes 393248 | tf_op jit(solution)/shard_map/ppermute | solution.py:284
  184.7 17.5 %fusion.6 = bf16[1024,3072]{1,0:T(8,128)(2,1)} fusion(f32[1024,3072]{1,0:T(8,128)} %get-tuple-element.90, bf16[1024,768]{0,1:T(8,128)(2,1)S(1)} %fusion.101, bf16[3072,768]{1,0:T(8,128)(2,1)S(1)} %bitcast.307), kind=kOutput, calls=%fused_computation.8 | convolution fusion | flops 4894752768 | bytes 25165824 | tf_op jit(solution)/shard_map/dot_general | solution.py:39
  202.2 9.0 %multiply_reduce_fusion.5 = (f32[1024]{0:T(1024)S(1)}, f32[1024]{0:T(1024)S(1)}, f32[1024,768]{0,1:T(8,128)S(1)}) fusion(f32[768]{0:T(1024)S(1)} %copy-done.68, f32[1024]{0:T(1024)S(1)} %copy-done.52, f32[1024,768]{0,1:T(8,128)S(1)} %copy-done.4, f32[1024]{0:T(1024)S(1)} %broadcast_multiply_fusion.5, bf16[1024,3072]{1,0:T(8,128)(2,1)} %fusion.6, ...), kind=kOutput, calls=%fused_computation.52 | convolution fusion | flops 4836554752 | bytes 17320960 | tf_op jit(solution)/shard_map/dot_general | solution.py:39
  215.1 7.8 %convolution_convert_fusion.1 = bf16[3072,384]{1,0:T(8,128)(2,1)} fusion(bf16[1024,3072]{1,0:T(8,128)(2,1)} %get-tuple-element.89, bf16[1024,768]{0,1:T(8,128)(2,1)S(1)} %fusion.101, s32[]{:T(128)S(6)} %select_n.377), kind=kOutput, calls=%fused_computation.17 | convolution fusion | flops 2417098752 | bytes 9437188 | tf_op jit(solution)/shard_map/dot_general | solution.py:43
  228.1 26.6 %enc_attend_back.1 = bf16[8,128,2304]{2,1,0:T(8,128)(2,1)} custom-call(bf16[8,128,2304]{2,1,0:T(8,128)(2,1)} %bitcast.288, bf16[8,128,768]{2,1,0:T(8,128)(2,1)} %bitcast.315), custom_call_target="tpu_custom_call" | custom-call | flops 4026531840 | bytes 11010048 | tf_op jit(solution)/shard_map/enc_attend_back/pallas_call | solution.py:149
  254.7 5.7 %convolution_convert_fusion.6 = bf16[768,1152]{1,0:T(8,128)(2,1)} fusion(bf16[1024,768]{0,1:T(8,128)(2,1)} %copy-done.31, bf16[1024,2304]{1,0:T(8,128)(2,1)} %bitcast.308, s32[]{:T(128)S(6)} %select_n.379), kind=kOutput, calls=%fused_computation.24 | convolution fusion | flops 1812824064 | bytes 5701636 | tf_op jit(solution)/shard_map/dot_general | solution.py:43
  302.2 18.2 %collective-permute-done.13 = bf16[2,2,96,1536]{3,2,1,0:T(8,128)(2,1)S(1)} collective-permute-done((bf16[2,2,96,1536]{3,2,1,0:T(8,128)(2,1)S(1)}, bf16[2,2,96,1536]{3,2,1,0:T(8,128)(2,1)S(1)}, u32[]{:S(2)}, u32[]{:S(2)}) %collective-permute-start.13) | collective-permute-done | bytes 1179680 | tf_op jit(solution)/shard_map/ppermute | solution.py:284
  349.1 11.7 %collective-permute-done.15 = bf16[96,1536]{1,0:T(8,128)(2,1)S(1)} collective-permute-done((bf16[96,1536]{1,0:T(8,128)(2,1)S(1)}, bf16[96,1536]{1,0:T(8,128)(2,1)S(1)}, u32[]{:S(2)}, u32[]{:S(2)}) %collective-permute-start.15) | collective-permute-done | bytes 294944 | tf_op jit(solution)/shard_map/ppermute | solution.py:284
  363.4 12.8 %collective-permute-done.6 = bf16[2,96,1536]{2,1,0:T(8,128)(2,1)S(1)} collective-permute-done((bf16[2,96,1536]{2,1,0:T(8,128)(2,1)S(1)}, bf16[2,96,1536]{2,1,0:T(8,128)(2,1)S(1)}, u32[]{:S(2)}, u32[]{:S(2)}) %collective-permute-start.6) | collective-permute-done | bytes 589856 | tf_op jit(solution)/shard_map/ppermute | solution.py:284
  377.1 27.0 %collective-permute-done.16 = bf16[96,1536]{1,0:T(8,128)(2,1)S(1)} collective-permute-done((bf16[96,1536]{1,0:T(8,128)(2,1)S(1)}, bf16[96,1536]{1,0:T(8,128)(2,1)S(1)}, u32[]{:S(2)}, u32[]{:S(2)}) %collective-permute-start.16) | collective-permute-done | bytes 294944 | tf_op jit(solution)/shard_map/ppermute | solution.py:284
  409.2 9.8 %collective-permute-done.7 = bf16[96,1536]{1,0:T(8,128)(2,1)S(1)} collective-permute-done((bf16[96,1536]{1,0:T(8,128)(2,1)S(1)}, bf16[96,1536]{1,0:T(8,128)(2,1)S(1)}, u32[]{:S(2)}, u32[]{:S(2)}) %collective-permute-start.7) | collective-permute-done | bytes 294944 | tf_op jit(solution)/shard_map/ppermute | solution.py:284
  436.4 6.6 %collective-permute-done.38 = bf16[2,48,1536]{2,1,0:T(8,128)(2,1)S(1)} collective-permute-done((bf16[2,48,1536]{2,1,0:T(8,128)(2,1)S(1)}, bf16[2,48,1536]{2,1,0:T(8,128)(2,1)S(1)}, u32[]{:S(2)}, u32[]{:S(2)}) %collective-permute-start.38) | collective-permute-done | bytes 294944 | tf_op jit(solution)/shard_map/ppermute | solution.py:284
  446.7 14.6 %collective-permute-done.39 = bf16[48,1536]{1,0:T(8,128)(2,1)S(1)} collective-permute-done((bf16[48,1536]{1,0:T(8,128)(2,1)S(1)}, bf16[48,1536]{1,0:T(8,128)(2,1)S(1)}, u32[]{:S(2)}, u32[]{:S(2)}) %collective-permute-start.39) | collective-permute-done | bytes 147488 | tf_op jit(solution)/shard_map/ppermute | solution.py:284
  468.6 13.0 %collective-permute-done.28 = bf16[384,384]{1,0:T(8,128)(2,1)S(1)} collective-permute-done((bf16[384,384]{1,0:T(8,128)(2,1)S(1)}, bf16[384,384]{1,0:T(8,128)(2,1)S(1)}, u32[]{:S(2)}, u32[]{:S(2)}) %collective-permute-start.28) | collective-permute-done | bytes 294944 | tf_op jit(solution)/shard_map/ppermute | solution.py:284
  492.5 6.5 %collective-permute-done.45 = bf16[96,1536]{1,0:T(8,128)(2,1)S(1)} collective-permute-done((bf16[96,1536]{1,0:T(8,128)(2,1)S(1)}, bf16[96,1536]{1,0:T(8,128)(2,1)S(1)}, u32[]{:S(2)}, u32[]{:S(2)}) %collective-permute-start.45) | collective-permute-done | bytes 294944 | tf_op jit(solution)/shard_map/ppermute | solution.py:284
  (481 shorter events, 239.5 us)
Async XLA Ops:
  155.9 132.0 %collective-permute-start.4 = (bf16[768,1152]{1,0:T(8,128)(2,1)}, bf16[768,1152]{1,0:T(8,128)(2,1)}, u32[]{:S(2)}, u32[]{:S(2)}) collective-permute-start(bf16[768,1152]{1,0:T(8,128)(2,1)} %convolution_convert_fusion.8), channel_id=1, source_target_pairs={{0,8},{8,0},{16,24},{24,16},{1,9},{9,1},{17,25},{25,17},{2,10},{10... | collective-permute-start | bytes 5308424 | tf_op jit(solution)/shard_map/ppermute | solution.py:284
  155.9 106.1 %collective-permute-start.3 = (bf16[768,384]{0,1:T(8,128)(2,1)}, bf16[768,384]{0,1:T(8,128)(2,1)}, u32[]{:S(2)}, u32[]{:S(2)}) collective-permute-start(bf16[768,384]{0,1:T(8,128)(2,1)} %convolution_convert_fusion.14), channel_id=1, source_target_pairs={{0,8},{8,0},{16,24},{24,16},{1,9},{9,1},{17,25},{25,17},{2,10},{10... | collective-permute-start | bytes 1769480 | tf_op jit(solution)/shard_map/ppermute | solution.py:284
  173.1 103.4 %collective-permute-start.12 = (bf16[768,768]{0,1:T(8,128)(2,1)}, bf16[768,768]{0,1:T(8,128)(2,1)}, u32[]{:S(2)}, u32[]{:S(2)}) collective-permute-start(bf16[768,768]{0,1:T(8,128)(2,1)} %fusion.36), channel_id=1, source_target_pairs={{0,8},{8,0},{16,24},{24,16},{1,9},{9,1},{17,25},{25,17},{2,10},{10... | collective-permute-start | bytes 3538952 | tf_op jit(solution)/shard_map/ppermute | solution.py:284
  181.7 84.8 %collective-permute-start.11 = (bf16[768,384]{0,1:T(8,128)(2,1)}, bf16[768,384]{0,1:T(8,128)(2,1)}, u32[]{:S(2)}, u32[]{:S(2)}) collective-permute-start(bf16[768,384]{0,1:T(8,128)(2,1)} %convolution_convert_fusion.12), channel_id=1, source_target_pairs={{0,8},{8,0},{16,24},{24,16},{1,9},{9,1},{17,25},{25,17},{2,10},{10... | collective-permute-start | bytes 1769480 | tf_op jit(solution)/shard_map/ppermute | solution.py:284
  181.7 87.9 %collective-permute-start.10 = (bf16[768,384]{0,1:T(8,128)(2,1)}, bf16[768,384]{0,1:T(8,128)(2,1)}, u32[]{:S(2)}, u32[]{:S(2)}) collective-permute-start(bf16[768,384]{0,1:T(8,128)(2,1)} %convolution_convert_fusion.13), channel_id=1, source_target_pairs={{0,8},{8,0},{16,24},{24,16},{1,9},{9,1},{17,25},{25,17},{2,10},{10... | collective-permute-start | bytes 1769480 | tf_op jit(solution)/shard_map/ppermute | solution.py:284
  266.5 31.2 %collective-permute-start.18 = (bf16[768,1536]{1,0:T(8,128)(2,1)}, bf16[768,1536]{1,0:T(8,128)(2,1)}, u32[]{:S(2)}, u32[]{:S(2)}) collective-permute-start(bf16[768,1536]{1,0:T(8,128)(2,1)} %convolution_convert_fusion.7), channel_id=1, source_target_pairs={{0,8},{8,0},{16,24},{24,16},{1,9},{9,1},{17,25},{25,17},{2,10},{10... | collective-permute-start | bytes 7077896 | tf_op jit(solution)/shard_map/ppermute | solution.py:284
  269.6 53.1 %collective-permute-start.25 = (bf16[3072,384]{1,0:T(8,128)(2,1)}, bf16[3072,384]{1,0:T(8,128)(2,1)}, u32[]{:S(2)}, u32[]{:S(2)}) collective-permute-start(bf16[3072,384]{1,0:T(8,128)(2,1)} %convolution_convert_fusion.2), channel_id=1, source_target_pairs={{0,8},{8,0},{16,24},{24,16},{1,9},{9,1},{17,25},{25,17},{2,10},{10... | collective-permute-start | bytes 7077896 | tf_op jit(solution)/shard_map/ppermute | solution.py:284
  276.6 57.0 %collective-permute-start.42 = (bf16[768,1536]{1,0:T(8,128)(2,1)}, bf16[768,1536]{1,0:T(8,128)(2,1)}, u32[]{:S(2)}, u32[]{:S(2)}) collective-permute-start(bf16[768,1536]{1,0:T(8,128)(2,1)} %convolution_convert_fusion.5), channel_id=1, source_target_pairs={{0,8},{8,0},{16,24},{24,16},{1,9},{9,1},{17,25},{25,17},{2,10},{10... | collective-permute-start | bytes 7077896 | tf_op jit(solution)/shard_map/ppermute | solution.py:284
  288.0 40.5 %collective-permute-start.48 = (bf16[3072,384]{1,0:T(8,128)(2,1)}, bf16[3072,384]{1,0:T(8,128)(2,1)S(1)}, u32[]{:S(2)}, u32[]{:S(2)}) collective-permute-start(bf16[3072,384]{1,0:T(8,128)(2,1)} %convolution_convert_fusion.1), channel_id=1, source_target_pairs={{0,8},{8,0},{16,24},{24,16},{1,9},{9,1},{17,25},{25,17},{2,10},{10... | collective-permute-start | bytes 7077896 | tf_op jit(solution)/shard_map/ppermute | solution.py:284
  291.4 28.9 %collective-permute-start.13 = (bf16[2,2,96,1536]{3,2,1,0:T(8,128)(2,1)S(1)}, bf16[2,2,96,1536]{3,2,1,0:T(8,128)(2,1)S(1)}, u32[]{:S(2)}, u32[]{:S(2)}) collective-permute-start(bf16[2,2,96,1536]{3,2,1,0:T(8,128)(2,1)S(1)} %dynamic-slice_bitcast_fusion), channel_id=1, source_target_pairs={{0,1},{1,0},{2,3},{3,2},{4,5},{5,4},{6,7},{7,6},{8,9},{9,8},{10,11... | collective-permute-start | bytes 3538952 | tf_op jit(solution)/shard_map/ppermute | solution.py:284
  297.8 47.8 %collective-permute-start.5 = (bf16[2,2,96,1536]{3,2,0,1:T(8,128)(2,1)S(1)}, bf16[2,2,96,1536]{3,2,0,1:T(8,128)(2,1)S(1)}, u32[]{:S(2)}, u32[]{:S(2)}) collective-permute-start(bf16[2,2,96,1536]{3,2,0,1:T(8,128)(2,1)S(1)} %bitcast.297), channel_id=1, source_target_pairs={{0,1},{1,0},{2,3},{3,2},{4,5},{5,4},{6,7},{7,6},{8,9},{9,8},{10,11... | collective-permute-start | bytes 3538952 | tf_op jit(solution)/shard_map/ppermute | solution.py:284
  320.3 41.9 %collective-permute-start.36 = (bf16[2,2,2,48,1536]{4,3,0,1,2:T(8,128)(2,1)S(1)}, bf16[2,2,2,48,1536]{4,3,0,1,2:T(8,128)(2,1)S(1)}, u32[]{:S(2)}, u32[]{:S(2)}) collective-permute-start(bf16[2,2,2,48,1536]{4,3,0,1,2:T(8,128)(2,1)S(1)} %bitcast.296), channel_id=1, source_target_pairs={{0,16},{8,24},{16,0},{24,8},{1,17},{9,25},{17,1},{25,9},{2,18},{10... | collective-permute-start | bytes 3538952 | tf_op jit(solution)/shard_map/ppermute | solution.py:284
  328.4 77.2 %collective-permute-start.19 = (bf16[2,2,2,48,1536]{4,3,0,1,2:T(8,128)(2,1)S(1)}, bf16[2,2,2,48,1536]{4,3,0,1,2:T(8,128)(2,1)S(1)}, u32[]{:S(2)}, u32[]{:S(2)}) collective-permute-start(bf16[2,2,2,48,1536]{4,3,0,1,2:T(8,128)(2,1)S(1)} %bitcast.294), channel_id=1, source_target_pairs={{0,16},{8,24},{16,0},{24,8},{1,17},{9,25},{17,1},{25,9},{2,18},{10... | collective-permute-start | bytes 3538952 | tf_op jit(solution)/shard_map/ppermute | solution.py:284
  333.6 75.1 %collective-permute-start.26 = (bf16[2,2,384,384]{3,2,0,1:T(8,128)(2,1)S(1)}, bf16[2,2,384,384]{3,2,0,1:T(8,128)(2,1)S(1)}, u32[]{:S(2)}, u32[]{:S(2)}) collective-permute-start(bf16[2,2,384,384]{3,2,0,1:T(8,128)(2,1)S(1)} %bitcast.295), channel_id=1, source_target_pairs={{0,1},{1,0},{2,3},{3,2},{4,5},{5,4},{6,7},{7,6},{8,9},{9,8},{10,11... | collective-permute-start | bytes 3538952 | tf_op jit(solution)/shard_map/ppermute | solution.py:284
  341.2 87.3 %collective-permute-start.43 = (bf16[2,2,96,1536]{3,2,0,1:T(8,128)(2,1)S(1)}, bf16[2,2,96,1536]{3,2,0,1:T(8,128)(2,1)S(1)}, u32[]{:S(2)}, u32[]{:S(2)}) collective-permute-start(bf16[2,2,96,1536]{3,2,0,1:T(8,128)(2,1)S(1)} %bitcast.293), channel_id=1, source_target_pairs={{0,1},{1,0},{2,3},{3,2},{4,5},{5,4},{6,7},{7,6},{8,9},{9,8},{10,11... | collective-permute-start | bytes 3538952 | tf_op jit(solution)/shard_map/ppermute | solution.py:284
  360.8 69.5 %collective-permute-start.49 = (bf16[2,2,2,192,384]{4,3,0,1,2:T(8,128)(2,1)S(1)}, bf16[2,2,2,192,384]{4,3,0,1,2:T(8,128)(2,1)S(1)}, u32[]{:S(2)}, u32[]{:S(2)}) collective-permute-start(bf16[2,2,2,192,384]{4,3,0,1,2:T(8,128)(2,1)S(1)} %bitcast.292), channel_id=1, source_target_pairs={{0,16},{8,24},{16,0},{24,8},{1,17},{9,25},{17,1},{25,9},{2,18},{10... | collective-permute-start | bytes 3538952 | tf_op jit(solution)/shard_map/ppermute | solution.py:284
  376.2 27.9 %collective-permute-start.16 = (bf16[96,1536]{1,0:T(8,128)(2,1)S(1)}, bf16[96,1536]{1,0:T(8,128)(2,1)S(1)}, u32[]{:S(2)}, u32[]{:S(2)}) collective-permute-start(bf16[96,1536]{1,0:T(8,128)(2,1)S(1)} %fusion.88), channel_id=1, source_target_pairs={{0,16},{8,24},{16,0},{24,8},{1,17},{9,25},{17,1},{25,9},{2,18},{10... | collective-permute-start | bytes 884744 | tf_op jit(solution)/shard_map/ppermute | solution.py:284
  404.1 22.8 %collective-permute-start.37 = (bf16[2,2,48,1536]{3,2,0,1:T(8,128)(2,1)S(1)}, bf16[2,2,48,1536]{3,2,0,1:T(8,128)(2,1)S(1)}, u32[]{:S(2)}, u32[]{:S(2)}) collective-permute-start(bf16[2,2,48,1536]{3,2,0,1:T(8,128)(2,1)S(1)} %dynamic-slice_bitcast_fusion.3), channel_id=1, source_target_pairs={{0,1},{1,0},{2,3},{3,2},{4,5},{5,4},{6,7},{7,6},{8,9},{9,8},{10,11... | collective-permute-start | bytes 1769480 | tf_op jit(solution)/shard_map/ppermute | solution.py:284
  420.3 22.8 %collective-permute-start.27 = (bf16[2,384,384]{2,1,0:T(8,128)(2,1)S(1)}, bf16[2,384,384]{2,1,0:T(8,128)(2,1)S(1)}, u32[]{:S(2)}, u32[]{:S(2)}) collective-permute-start(bf16[2,384,384]{2,1,0:T(8,128)(2,1)S(1)} %dynamic-slice_bitcast_fusion.4), channel_id=1, source_target_pairs={{0,2},{1,3},{2,0},{3,1},{4,6},{5,7},{6,4},{7,5},{8,10},{9,11},{10,... | collective-permute-start | bytes 1769480 | tf_op jit(solution)/shard_map/ppermute | solution.py:284
  430.3 53.7 %collective-permute-start.44 = (bf16[2,96,1536]{2,1,0:T(8,128)(2,1)S(1)}, bf16[2,96,1536]{2,1,0:T(8,128)(2,1)S(1)}, u32[]{:S(2)}, u32[]{:S(2)}) collective-permute-start(bf16[2,96,1536]{2,1,0:T(8,128)(2,1)S(1)} %dynamic-slice_bitcast_fusion.2), channel_id=1, source_target_pairs={{0,2},{1,3},{2,0},{3,1},{4,6},{5,7},{6,4},{7,5},{8,10},{9,11},{10,... | collective-permute-start | bytes 1769480 | tf_op jit(solution)/shard_map/ppermute | solution.py:284
  435.2 50.0 %collective-permute-start.50 = (bf16[2,2,192,384]{3,2,0,1:T(8,128)(2,1)S(1)}, bf16[2,2,192,384]{3,2,0,1:T(8,128)(2,1)S(1)}, u32[]{:S(2)}, u32[]{:S(2)}) collective-permute-start(bf16[2,2,192,384]{3,2,0,1:T(8,128)(2,1)S(1)} %dynamic-slice_bitcast_fusion.1), channel_id=1, source_target_pairs={{0,1},{1,0},{2,3},{3,2},{4,5},{5,4},{6,7},{7,6},{8,9},{9,8},{10,11... | collective-permute-start | bytes 1769480 | tf_op jit(solution)/shard_map/ppermute | solution.py:284
  436.1 29.6 %collective-permute-start.9 = (bf16[96,1536]{1,0:T(8,128)(2,1)S(1)}, bf16[96,1536]{1,0:T(8,128)(2,1)S(1)}, u32[]{:S(2)}, u32[]{:S(2)}) collective-permute-start(bf16[96,1536]{1,0:T(8,128)(2,1)S(1)} %add_convert_fusion.15), channel_id=1, source_target_pairs={{0,8},{8,0},{16,24},{24,16},{1,9},{9,1},{17,25},{25,17},{2,10},{10... | collective-permute-start | bytes 884744 | tf_op jit(solution)/shard_map/ppermute | solution.py:284
  443.0 21.7 %collective-permute-start.21 = (bf16[2,48,1536]{2,1,0:T(8,128)(2,1)S(1)}, bf16[2,48,1536]{2,1,0:T(8,128)(2,1)S(1)}, u32[]{:S(2)}, u32[]{:S(2)}) collective-permute-start(bf16[2,48,1536]{2,1,0:T(8,128)(2,1)S(1)} %dynamic-slice_bitcast_fusion.12), channel_id=1, source_target_pairs={{0,2},{1,3},{2,0},{3,1},{4,6},{5,7},{6,4},{7,5},{8,10},{9,11},{10,... | collective-permute-start | bytes 884744 | tf_op jit(solution)/shard_map/ppermute | solution.py:284
  491.9 25.6 %collective-permute-start.30 = (bf16[384,384]{1,0:T(8,128)(2,1)S(1)}, bf16[384,384]{1,0:T(8,128)(2,1)S(1)}, u32[]{:S(2)}, u32[]{:S(2)}) collective-permute-start(bf16[384,384]{1,0:T(8,128)(2,1)S(1)} %add_convert_fusion.13), channel_id=1, source_target_pairs={{0,8},{8,0},{16,24},{24,16},{1,9},{9,1},{17,25},{25,17},{2,10},{10... | collective-permute-start | bytes 884744 | tf_op jit(solution)/shard_map/ppermute | solution.py:284
  (128 other events, 1157.4 us)
